TPU v7x, 512 devices: a whole 4x8x8 slice. The times are simulated.
512 devices in a mesh: ia: 8 (over y_hi, x), ja: 16 (over z, core), ka: 4 (over y_lo).
Axes of the slice: x: 4, y: 8 (y_hi: 2, y_lo: 4; y = y_hi * 4 + y_lo), z: 8, core: 2. Of those that a mesh axis runs over, the one named last changes fastest.
Arguments:
- slab: float32 [256, 1024, 1024], P('ia', 'ja', 'ka'), may hold values from -8 to 8
- factor_two: float32 [1024, 48], P('ja'), may hold values from -0.1875 to 0.1875
- factor_three: float32 [1024, 48], P('ka'), may hold values from -0.1875 to 0.1875
Outputs:
- core: float32 [256, 2304], P('ia', ('ja', 'ka'))
- gram: float32 [256, 256], P('ia')
All inputs are finite; a program needn't handle non-finite values.
Results may differ from a plain program's by a relative error of at most 0.00007.
Values sent between devices are 32-bit elements; how exact they have to be, the bound alone decides.
No kernel may reach another device: no remote copies, remote signals or barrier semaphores. Data moves between devices by JAX's collectives and lax.ppermute only.
A program may use at most 64 MiB of HBM per device.

v0:
```python
import jax
import jax.numpy as jnp
from jax import lax
from jax.sharding import PartitionSpec as P


def on_device(slab, factor_two, factor_three):
    highest = lax.Precision.HIGHEST
    height, across, depth = slab.shape
    rank = factor_two.shape[1]
    middle = jnp.einsum("ijk,jr->irk", slab, factor_two, precision=highest)
    partial_value = jnp.einsum("irk,ks->irs", middle, factor_three, precision=highest)
    partial_value = partial_value.reshape(height, rank * rank)
    core = lax.psum_scatter(partial_value, ("ja", "ka"), scatter_dimension=1, tiled=True)
    terms = jnp.dot(
        core,
        lax.all_gather(core, "ia", axis=0, tiled=True).T,
        precision=highest,
        preferred_element_type=jnp.float32,
    )
    gram = lax.psum(terms, ("ja", "ka"))
    return (core, gram / (rank * rank))


def solution(mesh):
    placed = (P("ia", "ja", "ka"), P("ja", None), P("ka", None))
    return jax.shard_map(
        on_device,
        mesh=mesh,
        in_specs=placed,
        out_specs=(P("ia", ("ja", "ka")), P("ia", None)),
        check_vma=False,
    )
```

profile of v0, /device:TPU:1, one launch (start us, length us, event | category | flops | bytes accessed | tf_op | source)
XLA Modules:
  0.0 836.4 jit_solution(1312171259964248296)
XLA Ops:
  7.2 0.0 copy-start
  7.2 0.0 copy-start.2
  7.2 0.0 all-reduce.3.cloned.1.call-start
  7.2 1.5 copy-done
  8.8 2.1 fusion.3
  10.9 0.0 copy-done.2
  10.9 1.4 fusion
  12.3 1.0 reshape.7
  13.3 0.0 all-reduce.3.cloned.1.call-update
  13.3 1.3 dynamic-slice
  15.3 506.4 %all-reduce.3.cloned.1.call-done = f32[32,2304]{1,0:T(8,128)} async-done(((f32[32,2304]{1,0:T(8,128)}), f32[32,2304]{1,0:T(8,128)}) %all-reduce.3.cloned.1.call-update) | async-done | bytes 294928
  521.6 0.8 constant_dynamic-slice_fusion
  522.5 0.0 copy-start.1
  522.5 37.5 %all_gather.3 = f32[256,36]{1,0:T(8,128)S(1)} all-gather(f32[32,36]{1,0:T(8,128)S(1)} %constant_dynamic-slice_fusion), channel_id=1, replica_groups=mesh['ia'=8,'ja'=16,'ka'=4] {'ia'}, dimensions={0}, use_global_device_ids=true | all-gather | bytes 41472 | tf_op jit(solution)/shard_map/all_gather | solution.py:17
  560.0 0.2 fusion.5
  560.3 268.6 %psum.7 = f32[32,256]{1,0:T(8,128)S(1)} all-reduce(f32[32,256]{1,0:T(8,128)S(1)} %fusion.5), channel_id=1, replica_groups=mesh['ia'=8,'ja'=16,'ka'=4] {'ja','ka'}, use_global_device_ids=true, to_apply=%region_1.0 | all-reduce | flops 8192 | bytes 65536 | tf_op jit(solution)/shard_map/psum | solution.py:21
  828.9 0.6 broadcast_multiply_fusion
  829.5 0.0 copy-done.1
Async XLA Ops:
  7.2 1.6 copy-start
  7.2 3.7 copy-start.2
  7.2 514.4 %all-reduce.3.cloned.1.call-start = ((), (), s32[]{:S(2)}) async-start(), calls=%async_computation | async-start | bytes 589824
  522.5 307.1 %copy-start.1 = (f32[32,36]{1,0:T(8,128)}, f32[32,36]{1,0:T(8,128)S(1)}, u32[]{:S(2)}) copy-start(f32[32,36]{1,0:T(8,128)S(1)} %constant_dynamic-slice_fusion) | copy-start | bytes 13828
Sparse Core Ops, SparseCore 0:
  13.4 508.1 all-reduce.2
where the time goes:
time: 841 us; the launch traced here: 836 us
  waiting for transfers between devices  506 us (60%)
  blocking collectives  306 us (36%)
  between operations  14.7 us (2%)
    unnamed x2, waiting for transfers between devices  506 us
    psum x1, blocking collectives, on_device(): gram = lax.psum(terms, ('ja', 'ka'))  269 us
    all_gather x1, blocking collectives, on_device(): lax.all_gather(core, 'ia', axis=0, tiled=True)  37.5 us
  transfers between devices with their start and end apart: 1, of which 1 were waited for; matrix products, arithmetic and copies ran while one was open for 0% of the time, Pallas kernels for 0%

commit v1 on v0

v1 whole, which is shorter than its diff:
```python
import jax
import jax.numpy as jnp
from jax import lax
from jax.sharding import Mesh, PartitionSpec as P

HI = lax.Precision.HIGHEST


def on_device(slab, factor_two, factor_three):
    rows, _, _ = slab.shape
    rank = factor_two.shape[1]
    n_b = 64
    cols = rank * rank // n_b
    first = jnp.einsum("ijk,ks->jsi", slab, factor_three, precision=HI)
    partial_value = jnp.einsum("jr,jsi->rsi", factor_two, first, precision=HI)
    chunks = partial_value.reshape(n_b, 1, cols * rows)
    got = lax.all_to_all(chunks, ("z", "c", "l"), 0, 0, tiled=True)
    own = jnp.sum(got, axis=0)
    core = own.reshape(cols, rows).T
    sent = jnp.broadcast_to(own[None], (32, 1, cols * rows))
    every = lax.all_to_all(sent, ("h", "x", "l"), 0, 0, tiled=True)
    every = every.reshape(8, 4, cols, rows)
    me = lax.axis_index(("h", "x"))
    mine = lax.dynamic_index_in_dim(every, me, 0, keepdims=False)
    terms = jnp.einsum("lci,alcm->iam", mine, every, precision=HI).reshape(rows, 8 * rows)
    other = lax.ppermute(terms, "c", [(0, 1), (1, 0)])
    terms = terms + other
    parts = lax.all_to_all(jnp.broadcast_to(terms[None], (8,) + terms.shape), "z", 0, 0, tiled=True)
    gram = jnp.sum(parts, axis=0) / (rank * rank)
    return core, gram


def solution(mesh):
    fine = Mesh(mesh.devices.reshape(2, 4, 8, 2, 4), ("h", "x", "z", "c", "l"))
    placed = (P(("h", "x"), ("z", "c"), "l"), P(("z", "c"), None), P("l", None))
    return jax.shard_map(
        on_device,
        mesh=fine,
        in_specs=placed,
        out_specs=(P(("h", "x"), ("z", "c", "l")), P(("h", "x"), None)),
        check_vma=False,
    )
```

time: 841 us -> 81.9 us (0.10)
  waiting for transfers between devices: 506 us -> 22.3 us
  blocking collectives: 306 us -> 28.4 us
  starting transfers between devices: 0.04 us -> 15.4 us
  between operations: 14.7 us -> 0.73 us
    unnamed x2 -> x0, waiting for transfers between devices: 506 us -> none
    psum x1 -> x0, blocking collectives: 269 us -> none  [on_device(): gram = lax.psum(terms, ('ja', 'ka'))]
    all_gather x1 -> x0, blocking collectives: 37.5 us -> none  [on_device(): lax.all_gather(core, 'ia', axis=0, tiled=True)]
    all_to_all x0 -> x1, blocking collectives: none -> 28.4 us  [on_device(): got = lax.all_to_all(chunks, ('z', 'c', 'l'), 0, 0, tiled=True)]
    all_to_all x0 -> x2, waiting for transfers between devices: none -> 21.5 us  [the longest x1 11.5 us: on_device(): lax.all_to_all(jnp.broadcast_to(terms[None], (8,) + terms.shape), 'z', 0,...]
    all_to_all x0 -> x2, starting transfers between devices: none -> 10.4 us  [the longest x1 6.98 us: on_device(): every = lax.all_to_all(sent, ('h', 'x', 'l'), 0, 0, tiled=True)]
  transfers between devices with their start and end apart: 1 -> 3, of which waited for: 1 -> 3; matrix products, arithmetic and copies ran while one was open for 0% -> 1% of each run, Pallas kernels for 0% -> 0%
where the time goes in v1:
time: 81.9 us; the launch traced here: 81.4 us
  blocking collectives  28.4 us (35%)
  waiting for transfers between devices  22.3 us (27%)
  starting transfers between devices  15.4 us (19%)
  local copies, waits for them, and re-layouts  7.54 us (9%)
  matrix products  5.8 us (7%)
  other arithmetic  1.19 us (1%)
    all_to_all x1, blocking collectives, on_device(): got = lax.all_to_all(chunks, ('z', 'c', 'l'), 0, 0, tiled=True)  28.4 us
    all_to_all x1, waiting for transfers between devices, on_device(): lax.all_to_all(jnp.broadcast_to(terms[None], (8,) + terms.shape), 'z', 0,...  11.5 us
    all_to_all x1, waiting for transfers between devices, on_device(): every = lax.all_to_all(sent, ('h', 'x', 'l'), 0, 0, tiled=True)  9.97 us
    all_to_all x1, starting transfers between devices, on_device(): every = lax.all_to_all(sent, ('h', 'x', 'l'), 0, 0, tiled=True)  6.98 us
    ppermute x1, starting transfers between devices, on_device(): other = lax.ppermute(terms, 'c', [(0, 1), (1, 0)])  5.02 us
    dot_general x1, matrix products, on_device(): first = jnp.einsum('ijk,ks->jsi', slab, factor_three, precision=HI)  3.86 us
    all_to_all x1, starting transfers between devices, on_device(): lax.all_to_all(jnp.broadcast_to(terms[None], (8,) + terms.shape), 'z', 0,...  3.41 us
    unnamed x5, local copies, waits for them, and re-layouts  2.28 us
  transfers between devices with their start and end apart: 3, of which 3 were waited for; matrix products, arithmetic and copies ran while one was open for 1% of the time, Pallas kernels for 0%

profile of v1, /device:TPU:1, one launch (start us, length us, event | category | flops | bytes accessed | tf_op | source)
XLA Modules:
  0.0 81.4 jit_solution(333109654663479948)
XLA Ops:
  0.6 0.0 copy-start
  0.6 1.6 %copy-done = f32[32,64,256]{2,1,0:T(8,128)S(1)} copy-done((f32[32,64,256]{2,1,0:T(8,128)S(1)}, f32[32,64,256]{2,1,0:T(8,128)}, u32[]{:S(2)}) %copy-start) | copy-done | bytes 2097176
  2.2 0.0 copy-start.1
  2.2 3.9 %convolution_bitcast_fusion.1 = f32[64,48,32]{0,1,2:T(8,128)S(1)} fusion(f32[32,64,256]{2,1,0:T(8,128)S(1)} %copy-done, f32[256,48]{0,1:T(8,128)} %param.5), kind=kOutput, calls=%fused_computation.1 | convolution fusion | flops 301989888 | bytes 2539520 | tf_op jit(solution)/shard_map/ijk,ks->jsi/dot_general | solution.py:14
  6.1 0.0 copy-done.1
  6.1 1.6 %convolution_bitcast_fusion = f32[48,48,32]{0,1,2:T(8,128)} fusion(f32[64,48,32]{0,1,2:T(8,128)S(1)} %convolution_bitcast_fusion.1, f32[64,48]{0,1:T(8,128)S(1)} %copy-done.1), kind=kOutput, calls=%fused_computation | convolution fusion | flops 56623104 | bytes 700416 | tf_op jit(solution)/shard_map/jr,jsi->rsi/dot_general | solution.py:15
  7.8 1.8 %copy.17 = f32[48,48,32]{2,1,0:T(8,128)S(1)} copy(f32[48,48,32]{0,1,2:T(8,128)} %convolution_bitcast_fusion) | data formatting | bytes 589824 | tf_op jit(solution)/shard_map/jr,jsi->rsi/dot_general | solution.py:15
  9.5 1.2 %reshape.28 = f32[64,1,1152]{2,1,0:T(1,128)} reshape(f32[48,48,32]{2,1,0:T(8,128)S(1)} %copy.17) | data formatting | bytes 589824 | tf_op jit(solution)/shard_map/reshape | solution.py:16
  10.7 28.4 %all_to_all.15 = f32[64,1,1152]{2,1,0:T(1,128)S(1)} all-to-all(f32[64,1,1152]{2,1,0:T(1,128)} %reshape.28), channel_id=1, replica_groups=mesh['h'=2,'x'=4,'z'=8,'c'=2,'l'=4] {'z','c','l'}, dimensions={0} | all-to-all | bytes 589824 | tf_op jit(solution)/shard_map/all_to_all | solution.py:17
  39.2 0.2 reduce_sum.18
  39.4 0.7 broadcast_in_dim.4
  40.1 7.0 %all-to-all-start.1 = ((f32[32,1,1152]{2,1,0:T(1,128)}), f32[32,1,1152]{2,1,0:T(1,128)S(1)}, u32[]{:S(2)}, u32[]{:S(2)}) async-start(f32[32,1,1152]{2,1,0:T(1,128)} %broadcast_in_dim.4), calls=%async_computation.1 | async-start | bytes 294912 | tf_op jit(solution)/shard_map/all_to_all | solution.py:21
  47.1 10.0 %all-to-all-done.1 = f32[32,1,1152]{2,1,0:T(1,128)S(1)} async-done(((f32[32,1,1152]{2,1,0:T(1,128)}), f32[32,1,1152]{2,1,0:T(1,128)S(1)}, u32[]{:S(2)}, u32[]{:S(2)}) %all-to-all-start.1) | async-done | bytes 147488 | tf_op jit(solution)/shard_map/all_to_all | solution.py:21
  57.1 0.3 reduce.1
  57.4 0.2 reshape.24
  57.6 0.3 copy.23
  58.0 0.2 reshape.29
  58.2 0.3 convolution_bitcast_fusion.2
  58.5 5.0 %collective-permute-start = (f32[32,256]{1,0:T(8,128)S(1)}, f32[32,256]{1,0:T(8,128)S(1)}, u32[]{:S(2)}, u32[]{:S(2)}) collective-permute-start(f32[32,256]{1,0:T(8,128)S(1)} %convolution_bitcast_fusion.2), channel_id=1, source_target_pairs={{0,4},{4,0},{1,5},{5,1},{2,6},{6,2},{3,7},{7,3},{8,12},{12,8},{9,1... | collective-permute-start | bytes 98312 | tf_op jit(solution)/shard_map/ppermute | solution.py:26
  63.5 0.8 %collective-permute-done = f32[32,256]{1,0:T(8,128)S(1)} collective-permute-done((f32[32,256]{1,0:T(8,128)S(1)}, f32[32,256]{1,0:T(8,128)S(1)}, u32[]{:S(2)}, u32[]{:S(2)}) %collective-permute-start) | collective-permute-done | bytes 32800 | tf_op jit(solution)/shard_map/ppermute | solution.py:26
  64.4 0.7 broadcast_in_dim.5
  65.1 3.4 %all-to-all-start.2 = ((f32[8,32,256]{2,1,0:T(8,128)}), f32[8,32,256]{2,1,0:T(8,128)S(1)}, u32[]{:S(2)}, u32[]{:S(2)}) async-start(f32[8,32,256]{2,1,0:T(8,128)} %broadcast_in_dim.5), calls=%async_computation.2 | async-start | bytes 524288 | tf_op jit(solution)/shard_map/all_to_all | solution.py:28
  68.5 0.1 reshape.23
  68.6 0.7 copy.22
  69.3 11.5 %all-to-all-done.2 = f32[8,32,256]{2,1,0:T(8,128)S(1)} async-done(((f32[8,32,256]{2,1,0:T(8,128)}), f32[8,32,256]{2,1,0:T(8,128)S(1)}, u32[]{:S(2)}, u32[]{:S(2)}) %all-to-all-start.2) | async-done | bytes 262176 | tf_op jit(solution)/shard_map/all_to_all | solution.py:28
  80.8 0.6 broadcast_multiply_fusion
  (2 shorter events, 0.0 us)
Async XLA Ops:
  0.6 1.6 %copy-start = (f32[32,64,256]{2,1,0:T(8,128)S(1)}, f32[32,64,256]{2,1,0:T(8,128)}, u32[]{:S(2)}) copy-start(f32[32,64,256]{2,1,0:T(8,128)} %param.3) | copy-start | bytes 6291460
  2.2 3.9 %copy-start.1 = (f32[64,48]{0,1:T(8,128)S(1)}, f32[64,48]{0,1:T(8,128)}, u32[]{:S(2)}) copy-start(f32[64,48]{0,1:T(8,128)} %param.4) | copy-start | bytes 36868
  40.1 17.0 %all-to-all-start.1 = ((f32[32,1,1152]{2,1,0:T(1,128)}), f32[32,1,1152]{2,1,0:T(1,128)S(1)}, u32[]{:S(2)}, u32[]{:S(2)}) async-start(f32[32,1,1152]{2,1,0:T(1,128)} %broadcast_in_dim.4), calls=%async_computation.1 | async-start | bytes 294912 | tf_op jit(solution)/shard_map/all_to_all | solution.py:21
  58.5 5.9 %collective-permute-start = (f32[32,256]{1,0:T(8,128)S(1)}, f32[32,256]{1,0:T(8,128)S(1)}, u32[]{:S(2)}, u32[]{:S(2)}) collective-permute-start(f32[32,256]{1,0:T(8,128)S(1)} %convolution_bitcast_fusion.2), channel_id=1, source_target_pairs={{0,4},{4,0},{1,5},{5,1},{2,6},{6,2},{3,7},{7,3},{8,12},{12,8},{9,1... | collective-permute-start | bytes 98312 | tf_op jit(solution)/shard_map/ppermute | solution.py:26
  65.1 15.7 %all-to-all-start.2 = ((f32[8,32,256]{2,1,0:T(8,128)}), f32[8,32,256]{2,1,0:T(8,128)S(1)}, u32[]{:S(2)}, u32[]{:S(2)}) async-start(f32[8,32,256]{2,1,0:T(8,128)} %broadcast_in_dim.5), calls=%async_computation.2 | async-start | bytes 524288 | tf_op jit(solution)/shard_map/all_to_all | solution.py:28

commit v2 on v1

v2 whole, which is shorter than its diff:
```python
import functools
import jax
import jax.numpy as jnp
from jax import lax
from jax.experimental import pallas as pl
from jax.experimental.pallas import tpu as pltpu
from jax.sharding import Mesh, PartitionSpec as P

F32, BF16 = jnp.float32, jnp.bfloat16
NT = (((1,), (1,)), ((), ()))


def halves(x):
    high = x.astype(BF16)
    return high, (x - high.astype(F32)).astype(BF16)


def exact_nt(left, right):
    m = left.shape[0]
    lh, ll = halves(left)
    rh, rl = halves(right)
    both = lax.dot_general(jnp.concatenate([lh, ll], 0), rh, NT, preferred_element_type=F32)
    return both[:m] + both[m:] + lax.dot_general(lh, rl, NT, preferred_element_type=F32)


def project(slab_ref, two_ref, three_ref, out_ref, turned):
    step = pl.program_id(0)
    group, across, depth = slab_ref.shape
    rank = two_ref.shape[0]
    height = turned.shape[0] // rank
    first = exact_nt(three_ref[...], slab_ref[...].reshape(group * across, depth))
    for q in range(group):
        turned[pl.ds(step * group + q, rank, stride=height), :] = first[:, q * across : (q + 1) * across]

    @pl.when(step == pl.num_programs(0) - 1)
    def _():
        done = exact_nt(two_ref[...], turned[...])
        tiles = rank * height // 128
        for t in range(tiles):
            out_ref[pl.ds(t, rank, stride=tiles), :] = done[:, 128 * t : 128 * (t + 1)]


def front(slab, two, three, group=4):
    height, across, depth = slab.shape
    rank = two.shape[0]
    rows = rank * rank * height // 128
    return pl.pallas_call(
        project,
        grid=(height // group,),
        in_specs=[
            pl.BlockSpec((group, across, depth), lambda g: (g, 0, 0)),
            pl.BlockSpec((rank, across), lambda g: (0, 0)),
            pl.BlockSpec((rank, depth), lambda g: (0, 0)),
        ],
        out_specs=pl.BlockSpec((rows, 128), lambda g: (0, 0)),
        out_shape=jax.ShapeDtypeStruct((rows, 128), F32),
        scratch_shapes=[pltpu.VMEM((rank * height, across), F32)],
        name="project",
    )(slab, two, three)


def gather_sum(n_parts, copies, got_ref, core_ref, sent_ref, cols):
    rows = got_ref.shape[0] // n_parts
    own = got_ref[:rows, :]
    for b in range(1, n_parts):
        own = own + got_ref[rows * b : rows * (b + 1), :]
    for b in range(copies):
        sent_ref[rows * b : rows * (b + 1), :] = own
    height = core_ref.shape[0]
    per = 128 // height
    for q in range(per):
        cols[pl.ds(q, rows, stride=per), :] = own[:, height * q : height * (q + 1)]
    core_ref[...] = cols[...].T


def reduce_chunks(got, n_parts, copies, height):
    rows = got.shape[0] // n_parts
    n_cols = rows * 128 // height
    return pl.pallas_call(
        functools.partial(gather_sum, n_parts, copies),
        out_shape=(
            jax.ShapeDtypeStruct((height, n_cols), F32),
            jax.ShapeDtypeStruct((copies * rows, 128), F32),
        ),
        scratch_shapes=[pltpu.VMEM((n_cols, height), F32)],
        name="reduce_chunks",
    )(got)


def gram_terms(n_rows, height, axes, all_ref, out_ref):
    me = lax.axis_index(axes)
    per = 128 // height
    deep = all_ref.shape[0] // n_rows
    blocks = [all_ref[deep * a : deep * (a + 1), :] for a in range(n_rows)]
    mine = jnp.zeros_like(blocks[0])
    for a in range(n_rows):
        mine = jnp.where(me == a, blocks[a], mine)
    left = mine.T
    lane = lax.broadcasted_iota(jnp.int32, (height, 128), 1) // height
    folded = []
    for a in range(n_rows):
        z = exact_nt(left, blocks[a].T)
        u = jnp.zeros((height, 128), F32)
        for q in range(per):
            u = jnp.where(lane == q, z[height * q : height * (q + 1), :], u)
        shift = 64
        while shift >= height:
            u = u + pltpu.roll(u, shift, 1)
            shift //= 2
        folded.append(u)
    for t in range(n_rows // per):
        u = folded[t * per]
        for q in range(1, per):
            u = jnp.where(lane == q, folded[t * per + q], u)
        out_ref[:, 128 * t : 128 * (t + 1)] = u


def gram_part(every, n_rows, height, axes):
    return pl.pallas_call(
        functools.partial(gram_terms, n_rows, height, axes),
        out_shape=jax.ShapeDtypeStruct((height, n_rows * height), F32),
        name="gram_part",
    )(every)


def on_device(slab, factor_two, factor_three):
    height = slab.shape[0]
    rank = factor_two.shape[1]
    chunks = front(slab, factor_two.T, factor_three.T).reshape(64, 1, -1)
    got = lax.all_to_all(chunks, ("z", "c", "l"), 0, 0, tiled=True).reshape(-1, 128)
    core, sent = reduce_chunks(got, 64, 32, height)
    every = lax.all_to_all(sent.reshape(32, 1, -1), ("h", "x", "l"), 0, 0, tiled=True).reshape(-1, 128)
    terms = gram_part(every, 8, height, ("h", "x"))
    terms = terms + lax.ppermute(terms, "c", [(0, 1), (1, 0)])
    parts = lax.all_to_all(jnp.broadcast_to(terms[None], (8,) + terms.shape), "z", 0, 0, tiled=True)
    gram = jnp.sum(parts, axis=0) / (rank * rank)
    return core, gram


def solution(mesh):
    fine = Mesh(mesh.devices.reshape(2, 4, 8, 2, 4), ("h", "x", "z", "c", "l"))
    placed = (P(("h", "x"), ("z", "c"), "l"), P(("z", "c"), None), P("l", None))
    return jax.shard_map(
        on_device,
        mesh=fine,
        in_specs=placed,
        out_specs=(P(("h", "x"), ("z", "c", "l")), P(("h", "x"), None)),
        check_vma=False,
    )
```

time: 81.9 us -> 79.5 us (0.971)
  blocking collectives: 28.4 us -> 60.4 us
  waiting for transfers between devices: 22.3 us -> 1.05 us
  Pallas kernels: 0 us -> 10.5 us
  starting transfers between devices: 15.4 us -> 5.01 us
  local copies, waits for them, and re-layouts: 7.54 us -> 0.02 us
  matrix products: 5.8 us -> 0 us
    all_to_all x1 -> x3, blocking collectives: 28.4 us -> 60.4 us  [the longest x1 28.5 us: on_device(): lax.all_to_all(chunks, ('z', 'c', 'l'), 0, 0, tiled=True).reshape(-1, 128)]
    all_to_all x2 -> x0, waiting for transfers between devices: 21.5 us -> none  [the longest x1 11.5 us: on_device(): lax.all_to_all(jnp.broadcast_to(terms[None], (8,) + terms.shape), 'z', 0,...]
    pallas_call x0 -> x3, Pallas kernels: none -> 10.5 us  [the longest x1 6.51 us: front(): pl.pallas_call(project, grid=(height // group,), in_specs=[pl.BlockSpec((...]
    all_to_all x2 -> x0, starting transfers between devices: 10.4 us -> none  [the longest x1 6.98 us: on_device(): every = lax.all_to_all(sent, ('h', 'x', 'l'), 0, 0, tiled=True)]
    dot_general x3 -> x0, matrix products: 5.8 us -> none  [the longest x1 3.86 us: on_device(): first = jnp.einsum('ijk,ks->jsi', slab, factor_three, precision=HI)]
    dot_general x3 -> x0, local copies, waits for them, and re-layouts: 2.31 us -> none  [the longest x1 1.77 us: on_device(): partial_value = jnp.einsum('jr,jsi->rsi', factor_two, first, precision=HI)]
    unnamed x5 -> x0, local copies, waits for them, and re-layouts: 2.28 us -> none
    reshape x3 -> x0, local copies, waits for them, and re-layouts: 1.5 us -> none  [the longest x1 1.21 us: on_device(): chunks = partial_value.reshape(n_b, 1, cols * rows)]
  transfers between devices with their start and end apart: 3 -> 1, of which waited for: 3 -> 1; matrix products, arithmetic and copies ran while one was open for 1% -> 0% of each run, Pallas kernels for 0% -> 0%
where the time goes in v2:
time: 79.5 us; the launch traced here: 79 us
  blocking collectives  60.4 us (76%)
  Pallas kernels  10.5 us (13%)
  starting transfers between devices  5.01 us (6%)
  other arithmetic  1.4 us (2%)
  waiting for transfers between devices  1.05 us (1%)
    all_to_all x1, blocking collectives, on_device(): lax.all_to_all(chunks, ('z', 'c', 'l'), 0, 0, tiled=True).reshape(-1, 128)  28.5 us
    all_to_all x1, blocking collectives, on_device(): lax.all_to_all(sent.reshape(32, 1, -1), ('h', 'x', 'l'), 0, 0, tiled=True)  17.1 us
    all_to_all x1, blocking collectives, on_device(): lax.all_to_all(jnp.broadcast_to(terms[None], (8,) + terms.shape), 'z', 0,...  14.8 us
    pallas_call x1, Pallas kernels, front(): pl.pallas_call(project, grid=(height // group,), in_specs=[pl.BlockSpec((...  6.51 us
    ppermute x1, starting transfers between devices, on_device(): terms = terms + lax.ppermute(terms, 'c', [(0, 1), (1, 0)])  5.01 us
    pallas_call x1, Pallas kernels, gram_part(): pl.pallas_call(functools.partial(gram_terms, n_rows, height, axes), out_s...  2.23 us
    pallas_call x1, Pallas kernels, reduce_chunks(): pl.pallas_call(functools.partial(gather_sum, n_parts, copies), out_shape=...  1.78 us
  transfers between devices with their start and end apart: 1, of which 1 were waited for; matrix products, arithmetic and copies ran while one was open for 0% of the time, Pallas kernels for 0%

profile of v2, /device:TPU:1, one launch (start us, length us, event | category | flops | bytes accessed | tf_op | source)
XLA Modules:
  0.0 79.0 jit_solution(14423106487338348879)
XLA Ops:
  0.6 6.5 %project.1 = f32[576,128]{1,0:T(8,128)} custom-call(f32[32,64,256]{2,1,0:T(8,128)} %slab_ref.1, f32[48,64]{1,0:T(8,128)} %bitcast.11, f32[48,256]{1,0:T(8,128)} %bitcast.10), custom_call_target="tpu_custom_call" | custom-call | tf_op jit(solution)/shard_map/project/pallas_call | solution.py:47
  7.1 28.5 %all_to_all.15 = f32[64,1,1152]{2,1,0:T(1,128)} all-to-all(f32[64,1,1152]{2,1,0:T(1,128)} %bitcast.6), channel_id=1, replica_groups=mesh['h'=2,'x'=4,'z'=8,'c'=2,'l'=4] {'z','c','l'}, dimensions={0} | all-to-all | bytes 589824 | tf_op jit(solution)/shard_map/all_to_all | solution.py:130
  35.7 1.8 %reduce_chunks.1 = (f32[32,36]{1,0:T(8,128)}, f32[288,128]{1,0:T(8,128)}) custom-call(f32[576,128]{1,0:T(8,128)} %bitcast.7), custom_call_target="tpu_custom_call" | custom-call | tf_op jit(solution)/shard_map/reduce_chunks/pallas_call | solution.py:79
  37.5 17.1 %all_to_all.16 = f32[32,1,1152]{2,1,0:T(1,128)} all-to-all(f32[32,1,1152]{2,1,0:T(1,128)} %bitcast.9), channel_id=1, replica_groups=mesh['h'=2,'x'=4,'z'=8,'c'=2,'l'=4] {'h','x','l'}, dimensions={0} | all-to-all | bytes 294912 | tf_op jit(solution)/shard_map/all_to_all | solution.py:132
  54.5 2.2 %gram_part.1 = f32[32,256]{1,0:T(8,128)} custom-call(f32[288,128]{1,0:T(8,128)} %bitcast.8), custom_call_target="tpu_custom_call" | custom-call | tf_op jit(solution)/shard_map/gram_part/pallas_call | solution.py:119
  56.8 5.0 %collective-permute-start = (f32[32,256]{1,0:T(8,128)}, f32[32,256]{1,0:T(8,128)S(1)}, u32[]{:S(2)}, u32[]{:S(2)}) collective-permute-start(f32[32,256]{1,0:T(8,128)} %gram_part.1), channel_id=1, source_target_pairs={{0,4},{4,0},{1,5},{5,1},{2,6},{6,2},{3,7},{7,3},{8,12},{12,8},{9,1... | collective-permute-start | bytes 98312 | tf_op jit(solution)/shard_map/ppermute | solution.py:134
  61.8 1.0 %collective-permute-done = f32[32,256]{1,0:T(8,128)S(1)} collective-permute-done((f32[32,256]{1,0:T(8,128)}, f32[32,256]{1,0:T(8,128)S(1)}, u32[]{:S(2)}, u32[]{:S(2)}) %collective-permute-start) | collective-permute-done | bytes 32800 | tf_op jit(solution)/shard_map/ppermute | solution.py:134
  62.8 0.8 add.3
  63.6 14.8 %all_to_all.17 = f32[8,32,256]{2,1,0:T(8,128)S(1)} all-to-all(f32[8,32,256]{2,1,0:T(8,128)S(1)} %broadcast_in_dim.2), channel_id=1, replica_groups=mesh['h'=2,'x'=4,'z'=8,'c'=2,'l'=4] {'z'}, dimensions={0} | all-to-all | bytes 524288 | tf_op jit(solution)/shard_map/all_to_all | solution.py:135
  78.4 0.6 broadcast_multiply_fusion
  (2 shorter events, 0.0 us)
Async XLA Ops:
  56.8 6.1 %collective-permute-start = (f32[32,256]{1,0:T(8,128)}, f32[32,256]{1,0:T(8,128)S(1)}, u32[]{:S(2)}, u32[]{:S(2)}) collective-permute-start(f32[32,256]{1,0:T(8,128)} %gram_part.1), channel_id=1, source_target_pairs={{0,4},{4,0},{1,5},{5,1},{2,6},{6,2},{3,7},{7,3},{8,12},{12,8},{9,1... | collective-permute-start | bytes 98312 | tf_op jit(solution)/shard_map/ppermute | solution.py:134

commit v3 on v2

--- a/solution.py
+++ b/solution.py
@@ -40,7 +40,7 @@
             out_ref[pl.ds(t, rank, stride=tiles), :] = done[:, 128 * t : 128 * (t + 1)]
 
 
-def front(slab, two, three, group=4):
+def front(slab, two, three, group=16):
     height, across, depth = slab.shape
     rank = two.shape[0]
     rows = rank * rank * height // 128
@@ -53,19 +53,28 @@
             pl.BlockSpec((rank, depth), lambda g: (0, 0)),
         ],
         out_specs=pl.BlockSpec((rows, 128), lambda g: (0, 0)),
-        out_shape=jax.ShapeDtypeStruct((rows, 128), F32),
+        out_shape=pltpu.VMEM((rows, 128), F32),
         scratch_shapes=[pltpu.VMEM((rank * height, across), F32)],
+        compiler_params=pltpu.CompilerParams(vmem_limit_bytes=16 << 20),
         name="project",
-    )(slab, two, three)
+    )(*(pltpu.with_memory_space_constraint(x, pltpu.HBM) for x in (slab, two, three)))
 
 
-def gather_sum(n_parts, copies, got_ref, core_ref, sent_ref, cols):
+def gather_sum(n_parts, copies, got_ref, core_ref, sent_ref, cols, pattern):
     rows = got_ref.shape[0] // n_parts
-    own = got_ref[:rows, :]
-    for b in range(1, n_parts):
-        own = own + got_ref[rows * b : rows * (b + 1), :]
-    for b in range(copies):
-        sent_ref[rows * b : rows * (b + 1), :] = own
+    wide = 8 * rows
+    total = got_ref[:wide, :]
+    for b in range(1, n_parts // 8):
+        total = total + got_ref[wide * b : wide * (b + 1), :]
+    pattern[...] = total
+    own = pattern[:rows, :]
+    for b in range(1, 8):
+        own = own + pattern[rows * b : rows * (b + 1), :]
+    for b in range(8):
+        pattern[rows * b : rows * (b + 1), :] = own
+    total = pattern[...]
+    for b in range(copies // 8):
+        sent_ref[wide * b : wide * (b + 1), :] = total
     height = core_ref.shape[0]
     per = 128 // height
     for q in range(per):
@@ -80,11 +89,12 @@
         functools.partial(gather_sum, n_parts, copies),
         out_shape=(
             jax.ShapeDtypeStruct((height, n_cols), F32),
-            jax.ShapeDtypeStruct((copies * rows, 128), F32),
+            pltpu.VMEM((copies * rows, 128), F32),
         ),
-        scratch_shapes=[pltpu.VMEM((n_cols, height), F32)],
+        scratch_shapes=[pltpu.VMEM((n_cols, height), F32), pltpu.VMEM((8 * rows, 128), F32)],
+        compiler_params=pltpu.CompilerParams(vmem_limit_bytes=4 << 20),
         name="reduce_chunks",
-    )(got)
+    )(pltpu.with_memory_space_constraint(got, pltpu.VMEM))
 
 
 def gram_terms(n_rows, height, axes, all_ref, out_ref):
@@ -95,11 +105,14 @@
     mine = jnp.zeros_like(blocks[0])
     for a in range(n_rows):
         mine = jnp.where(me == a, blocks[a], mine)
-    left = mine.T
+    lh, ll = halves(mine.T)
+    rh, rl = halves(jnp.concatenate(blocks, 1))
+    both = jnp.dot(jnp.concatenate([lh, ll], 0), rh, preferred_element_type=F32)
+    low = jnp.dot(lh, rl, preferred_element_type=F32)
     lane = lax.broadcasted_iota(jnp.int32, (height, 128), 1) // height
     folded = []
     for a in range(n_rows):
-        z = exact_nt(left, blocks[a].T)
+        z = both[:128, 128 * a : 128 * (a + 1)] + both[128:, 128 * a : 128 * (a + 1)] + low[:, 128 * a : 128 * (a + 1)]
         u = jnp.zeros((height, 128), F32)
         for q in range(per):
             u = jnp.where(lane == q, z[height * q : height * (q + 1), :], u)
@@ -118,9 +131,10 @@
 def gram_part(every, n_rows, height, axes):
     return pl.pallas_call(
         functools.partial(gram_terms, n_rows, height, axes),
-        out_shape=jax.ShapeDtypeStruct((height, n_rows * height), F32),
+        out_shape=pltpu.VMEM((height, n_rows * height), F32),
+        compiler_params=pltpu.CompilerParams(vmem_limit_bytes=4 << 20),
         name="gram_part",
-    )(every)
+    )(pltpu.with_memory_space_constraint(every, pltpu.VMEM))
 
 
 def on_device(slab, factor_two, factor_three):

time: 79.5 us -> 71.4 us (0.90)
  Pallas kernels: 10.5 us -> 4.25 us
    pallas_call x1, Pallas kernels: 6.51 us -> 2.89 us  [front(): pl.pallas_call(project, grid=(height // group,), in_specs=[pl.BlockSpec((...]
    pallas_call x1, Pallas kernels: 2.23 us -> 0.57 us  [gram_part(): pl.pallas_call(functools.partial(gram_terms, n_rows, height, axes), out_s...]
    pallas_call x1, Pallas kernels: 1.78 us -> 0.78 us  [reduce_chunks(): pl.pallas_call(functools.partial(gather_sum, n_parts, copies), out_shape=...]
where the time goes in v3:
time: 71.4 us; the launch traced here: 71.2 us
  blocking collectives  59.7 us (84%)
  starting transfers between devices  5.02 us (7%)
  Pallas kernels  4.25 us (6%)
  waiting for transfers between devices  0.84 us (1%)
    all_to_all x1, blocking collectives, on_device(): lax.all_to_all(chunks, ('z', 'c', 'l'), 0, 0, tiled=True).reshape(-1, 128)  28.3 us
    all_to_all x1, blocking collectives, on_device(): lax.all_to_all(sent.reshape(32, 1, -1), ('h', 'x', 'l'), 0, 0, tiled=True)  16.7 us
    all_to_all x1, blocking collectives, on_device(): lax.all_to_all(jnp.broadcast_to(terms[None], (8,) + terms.shape), 'z', 0,...  14.8 us
    ppermute x1, starting transfers between devices, on_device(): terms = terms + lax.ppermute(terms, 'c', [(0, 1), (1, 0)])  5.02 us
    pallas_call x1, Pallas kernels, front(): pl.pallas_call(project, grid=(height // group,), in_specs=[pl.BlockSpec((...  2.89 us
  transfers between devices with their start and end apart: 1, of which 1 were waited for; matrix products, arithmetic and copies ran while one was open for 0% of the time, Pallas kernels for 0%

profile of v3, /device:TPU:1, one launch (start us, length us, event | category | flops | bytes accessed | tf_op | source)
XLA Modules:
  0.0 71.2 jit_solution(11695305867864822360)
XLA Ops:
  0.6 2.9 %project.1 = f32[576,128]{1,0:T(8,128)S(1)} custom-call(f32[32,64,256]{2,1,0:T(8,128)} %slab_ref.1, f32[48,64]{1,0:T(8,128)} %bitcast.11, f32[48,256]{1,0:T(8,128)} %bitcast.10), custom_call_target="tpu_custom_call" | custom-call | tf_op jit(solution)/shard_map/project/pallas_call | solution.py:47
  3.5 28.3 %all_to_all.15 = f32[64,1,1152]{2,1,0:T(1,128)S(1)} all-to-all(f32[64,1,1152]{2,1,0:T(1,128)S(1)} %bitcast.6), channel_id=1, replica_groups=mesh['h'=2,'x'=4,'z'=8,'c'=2,'l'=4] {'z','c','l'}, dimensions={0} | all-to-all | bytes 589824 | tf_op jit(solution)/shard_map/all_to_all | solution.py:144
  31.8 0.8 %reduce_chunks.1 = (f32[32,36]{1,0:T(8,128)}, f32[288,128]{1,0:T(8,128)S(1)}) custom-call(f32[576,128]{1,0:T(8,128)S(1)} %bitcast.7), custom_call_target="tpu_custom_call" | custom-call | tf_op jit(solution)/shard_map/reduce_chunks/pallas_call | solution.py:88
  32.6 16.7 %all_to_all.16 = f32[32,1,1152]{2,1,0:T(1,128)S(1)} all-to-all(f32[32,1,1152]{2,1,0:T(1,128)S(1)} %bitcast.9), channel_id=1, replica_groups=mesh['h'=2,'x'=4,'z'=8,'c'=2,'l'=4] {'h','x','l'}, dimensions={0} | all-to-all | bytes 294912 | tf_op jit(solution)/shard_map/all_to_all | solution.py:146
  49.3 0.6 gram_part.1
  49.9 5.0 %collective-permute-start = (f32[32,256]{1,0:T(8,128)S(1)}, f32[32,256]{1,0:T(8,128)S(1)}, u32[]{:S(2)}, u32[]{:S(2)}) collective-permute-start(f32[32,256]{1,0:T(8,128)S(1)} %gram_part.1), channel_id=1, source_target_pairs={{0,4},{4,0},{1,5},{5,1},{2,6},{6,2},{3,7},{7,3},{8,12},{12,8},{9,1... | collective-permute-start | bytes 98312 | tf_op jit(solution)/shard_map/ppermute | solution.py:148
  54.9 0.8 %collective-permute-done = f32[32,256]{1,0:T(8,128)S(1)} collective-permute-done((f32[32,256]{1,0:T(8,128)S(1)}, f32[32,256]{1,0:T(8,128)S(1)}, u32[]{:S(2)}, u32[]{:S(2)}) %collective-permute-start) | collective-permute-done | bytes 32800 | tf_op jit(solution)/shard_map/ppermute | solution.py:148
  55.8 14.8 %all_to_all.17 = f32[8,32,256]{2,1,0:T(8,128)S(1)} all-to-all(f32[8,32,256]{2,1,0:T(8,128)S(1)} %broadcast_in_dim.2), channel_id=1, replica_groups=mesh['h'=2,'x'=4,'z'=8,'c'=2,'l'=4] {'z'}, dimensions={0} | all-to-all | bytes 524288 | tf_op jit(solution)/shard_map/all_to_all | solution.py:149
  70.6 0.6 broadcast_multiply_fusion
  (3 shorter events, 0.0 us)
Async XLA Ops:
  49.9 5.9 %collective-permute-start = (f32[32,256]{1,0:T(8,128)S(1)}, f32[32,256]{1,0:T(8,128)S(1)}, u32[]{:S(2)}, u32[]{:S(2)}) collective-permute-start(f32[32,256]{1,0:T(8,128)S(1)} %gram_part.1), channel_id=1, source_target_pairs={{0,4},{4,0},{1,5},{5,1},{2,6},{6,2},{3,7},{7,3},{8,12},{12,8},{9,1... | collective-permute-start | bytes 98312 | tf_op jit(solution)/shard_map/ppermute | solution.py:148

commit v4 on v3

--- a/solution.py
+++ b/solution.py
@@ -34,10 +34,11 @@
 
     @pl.when(step == pl.num_programs(0) - 1)
     def _():
-        done = exact_nt(two_ref[...], turned[...])
+        two = two_ref[...]
+        done = exact_nt(jnp.concatenate([two[r : r + 1] for r in range(rank - 1, -1, -1)], 0), turned[...])
         tiles = rank * height // 128
         for t in range(tiles):
-            out_ref[pl.ds(t, rank, stride=tiles), :] = done[:, 128 * t : 128 * (t + 1)]
+            out_ref[pl.ds(tiles - 1 - t, rank, stride=tiles), :] = done[:, 128 * t : 128 * (t + 1)]
 
 
 def front(slab, two, three, group=16):
@@ -78,7 +79,9 @@
     height = core_ref.shape[0]
     per = 128 // height
     for q in range(per):
-        cols[pl.ds(q, rows, stride=per), :] = own[:, height * q : height * (q + 1)]
+        for m in range(rows):
+            at = per * (rows - 1 - m) + q
+            cols[at : at + 1, :] = own[m : m + 1, height * q : height * (q + 1)]
     core_ref[...] = cols[...].T
 
 
@@ -101,7 +104,7 @@
     me = lax.axis_index(axes)
     per = 128 // height
     deep = all_ref.shape[0] // n_rows
-    blocks = [all_ref[deep * a : deep * (a + 1), :] for a in range(n_rows)]
+    blocks = [all_ref[deep * a : deep * (a + 1), :] for a in range(n_rows)][::-1]
     mine = jnp.zeros_like(blocks[0])
     for a in range(n_rows):
         mine = jnp.where(me == a, blocks[a], mine)
@@ -141,12 +144,12 @@
     height = slab.shape[0]
     rank = factor_two.shape[1]
     chunks = front(slab, factor_two.T, factor_three.T).reshape(64, 1, -1)
-    got = lax.all_to_all(chunks, ("z", "c", "l"), 0, 0, tiled=True).reshape(-1, 128)
+    got = lax.all_to_all(chunks, ("z", "c", "l"), 0, 0, tiled=True, axis_index_groups=[list(range(63, -1, -1))]).reshape(-1, 128)
     core, sent = reduce_chunks(got, 64, 32, height)
-    every = lax.all_to_all(sent.reshape(32, 1, -1), ("h", "x", "l"), 0, 0, tiled=True).reshape(-1, 128)
+    every = lax.all_to_all(sent.reshape(32, 1, -1), ("h", "x", "l"), 0, 0, tiled=True, axis_index_groups=[list(range(31, -1, -1))]).reshape(-1, 128)
     terms = gram_part(every, 8, height, ("h", "x"))
     terms = terms + lax.ppermute(terms, "c", [(0, 1), (1, 0)])
-    parts = lax.all_to_all(jnp.broadcast_to(terms[None], (8,) + terms.shape), "z", 0, 0, tiled=True)
+    parts = lax.all_to_all(jnp.broadcast_to(terms[None], (8,) + terms.shape), "z", 0, 0, tiled=True, axis_index_groups=[[7, 6, 5, 4, 3, 2, 1, 0]])
     gram = jnp.sum(parts, axis=0) / (rank * rank)
     return core, gram
 

time: 71.4 us -> 62.8 us (0.88); the launches traced: 71.2 us -> 61.8 us
  blocking collectives: 59.7 us -> 51.4 us
  starting transfers between devices: 5.02 us -> 3.92 us
    all_to_all x2, blocking collectives: 45 us -> 40.5 us  [the longest x1 25.9 us: on_device(): lax.all_to_all(chunks, ('z', 'c', 'l'), 0, 0, tiled=True, axis_index_grou...]
    all_to_all x1, blocking collectives: 14.8 us -> 10.9 us  [on_device(): lax.all_to_all(jnp.broadcast_to(terms[None], (8,) + terms.shape), 'z', 0,...]
    ppermute x1, starting transfers between devices: 5.02 us -> 3.92 us  [on_device(): terms = terms + lax.ppermute(terms, 'c', [(0, 1), (1, 0)])]
where the time goes in v4:
time: 62.8 us; the launch traced here: 61.8 us
  blocking collectives  51.4 us (82%)
  Pallas kernels  4.25 us (7%)
  starting transfers between devices  3.92 us (6%)
  waiting for transfers between devices  0.84 us (1%)
  between operations  0.66 us (1%)
  other arithmetic  0.64 us (1%)
    all_to_all x1, blocking collectives, on_device(): lax.all_to_all(chunks, ('z', 'c', 'l'), 0, 0, tiled=True, axis_index_grou...  25.9 us
    all_to_all x1, blocking collectives, on_device(): lax.all_to_all(sent.reshape(32, 1, -1), ('h', 'x', 'l'), 0, 0, tiled=True...  14.6 us
    all_to_all x1, blocking collectives, on_device(): lax.all_to_all(jnp.broadcast_to(terms[None], (8,) + terms.shape), 'z', 0,...  10.9 us
    ppermute x1, starting transfers between devices, on_device(): terms = terms + lax.ppermute(terms, 'c', [(0, 1), (1, 0)])  3.92 us
    pallas_call x1, Pallas kernels, front(): pl.pallas_call(project, grid=(height // group,), in_specs=[pl.BlockSpec((...  2.89 us
  transfers between devices with their start and end apart: 1, of which 1 were waited for; matrix products, arithmetic and copies ran while one was open for 0% of the time, Pallas kernels for 0%

profile of v4, /device:TPU:1, one launch (start us, length us, event | category | flops | bytes accessed | tf_op | source)
XLA Modules:
  0.0 61.8 jit_solution(16595055009075691889)
XLA Ops:
  0.6 2.9 %project.1 = f32[576,128]{1,0:T(8,128)S(1)} custom-call(f32[32,64,256]{2,1,0:T(8,128)} %slab_ref.1, f32[48,64]{1,0:T(8,128)} %bitcast.11, f32[48,256]{1,0:T(8,128)} %bitcast.10), custom_call_target="tpu_custom_call" | custom-call | tf_op jit(solution)/shard_map/project/pallas_call | solution.py:48
  3.5 25.9 %all_to_all.15 = f32[64,1,1152]{2,1,0:T(1,128)S(1)} all-to-all(f32[64,1,1152]{2,1,0:T(1,128)S(1)} %bitcast.6), channel_id=1, replica_groups={{63,62,61,60,59,58,57,56,55,54,53,52,51,50,49,48,47,46,45,44,43,42,41,4..., dimensions={0} | all-to-all | bytes 589824 | tf_op jit(solution)/shard_map/all_to_all | solution.py:147
  29.5 0.8 %reduce_chunks.1 = (f32[32,36]{1,0:T(8,128)}, f32[288,128]{1,0:T(8,128)S(1)}) custom-call(f32[576,128]{1,0:T(8,128)S(1)} %bitcast.7), custom_call_target="tpu_custom_call" | custom-call | tf_op jit(solution)/shard_map/reduce_chunks/pallas_call | solution.py:91
  30.2 14.6 %all_to_all.16 = f32[32,1,1152]{2,1,0:T(1,128)S(1)} all-to-all(f32[32,1,1152]{2,1,0:T(1,128)S(1)} %bitcast.9), channel_id=1, replica_groups={{451,450,449,448,387,386,385,384,323,322,321,320,259,258,257,256,195,19..., dimensions={0} | all-to-all | bytes 294912 | tf_op jit(solution)/shard_map/all_to_all | solution.py:149
  44.9 0.6 gram_part.1
  45.4 3.9 %collective-permute-start = (f32[32,256]{1,0:T(8,128)S(1)}, f32[32,256]{1,0:T(8,128)S(1)}, u32[]{:S(2)}, u32[]{:S(2)}) collective-permute-start(f32[32,256]{1,0:T(8,128)S(1)} %gram_part.1), channel_id=1, source_target_pairs={{0,4},{4,0},{1,5},{5,1},{2,6},{6,2},{3,7},{7,3},{8,12},{12,8},{9,1... | collective-permute-start | bytes 98312 | tf_op jit(solution)/shard_map/ppermute | solution.py:151
  49.4 0.8 %collective-permute-done = f32[32,256]{1,0:T(8,128)S(1)} collective-permute-done((f32[32,256]{1,0:T(8,128)S(1)}, f32[32,256]{1,0:T(8,128)S(1)}, u32[]{:S(2)}, u32[]{:S(2)}) %collective-permute-start) | collective-permute-done | bytes 32800 | tf_op jit(solution)/shard_map/ppermute | solution.py:151
  50.2 10.9 %all_to_all.17 = f32[8,32,256]{2,1,0:T(8,128)S(1)} all-to-all(f32[8,32,256]{2,1,0:T(8,128)S(1)} %broadcast_in_dim.2), channel_id=1, replica_groups={{56,48,40,32,24,16,8,0},{57,49,41,33,25,17,9,1},{58,50,42,34,26,18,10,2..., dimensions={0} | all-to-all | bytes 524288 | tf_op jit(solution)/shard_map/all_to_all | solution.py:152
  61.2 0.6 %broadcast_multiply_fusion = f32[32,256]{1,0:T(8,128)} fusion(f32[32,256]{1,0:T(8,128)S(1)} %reduce_sum.9), kind=kLoop, calls=%fused_computation | loop fusion | flops 8192 | bytes 65536 | tf_op jit(solution)/shard_map/div | solution.py:153
  (3 shorter events, 0.0 us)
Async XLA Ops:
  45.4 4.8 %collective-permute-start = (f32[32,256]{1,0:T(8,128)S(1)}, f32[32,256]{1,0:T(8,128)S(1)}, u32[]{:S(2)}, u32[]{:S(2)}) collective-permute-start(f32[32,256]{1,0:T(8,128)S(1)} %gram_part.1), channel_id=1, source_target_pairs={{0,4},{4,0},{1,5},{5,1},{2,6},{6,2},{3,7},{7,3},{8,12},{12,8},{9,1... | collective-permute-start | bytes 98312 | tf_op jit(solution)/shard_map/ppermute | solution.py:151

commit v5 on v4

--- a/solution.py
+++ b/solution.py
@@ -61,7 +61,7 @@
     )(*(pltpu.with_memory_space_constraint(x, pltpu.HBM) for x in (slab, two, three)))
 
 
-def gather_sum(n_parts, copies, got_ref, core_ref, sent_ref, cols, pattern):
+def gather_sum(n_parts, copies, got_ref, sent_ref, pattern):
     rows = got_ref.shape[0] // n_parts
     wide = 8 * rows
     total = got_ref[:wide, :]
@@ -76,8 +76,13 @@
     total = pattern[...]
     for b in range(copies // 8):
         sent_ref[wide * b : wide * (b + 1), :] = total
-    height = core_ref.shape[0]
+
+
+def format_core(sent_ref, core_ref, cols):
+    height, n_cols = core_ref.shape
     per = 128 // height
+    rows = n_cols // per
+    own = sent_ref[:rows, :]
     for q in range(per):
         for m in range(rows):
             at = per * (rows - 1 - m) + q
@@ -85,16 +90,23 @@
     core_ref[...] = cols[...].T
 
 
-def reduce_chunks(got, n_parts, copies, height):
+def core_block(sent, height, n_cols):
+    return pl.pallas_call(
+        format_core,
+        out_shape=jax.ShapeDtypeStruct((height, n_cols), F32),
+        scratch_shapes=[pltpu.VMEM((n_cols, height), F32)],
+        compiler_params=pltpu.CompilerParams(vmem_limit_bytes=4 << 20),
+        cost_estimate=pl.CostEstimate(flops=1 << 20, bytes_accessed=1 << 21, transcendentals=0),
+        name="core_block",
+    )(pltpu.with_memory_space_constraint(sent, pltpu.VMEM))
+
+
+def reduce_chunks(got, n_parts, copies):
     rows = got.shape[0] // n_parts
-    n_cols = rows * 128 // height
     return pl.pallas_call(
         functools.partial(gather_sum, n_parts, copies),
-        out_shape=(
-            jax.ShapeDtypeStruct((height, n_cols), F32),
-            pltpu.VMEM((copies * rows, 128), F32),
-        ),
-        scratch_shapes=[pltpu.VMEM((n_cols, height), F32), pltpu.VMEM((8 * rows, 128), F32)],
+        out_shape=pltpu.VMEM((copies * rows, 128), F32),
+        scratch_shapes=[pltpu.VMEM((8 * rows, 128), F32)],
         compiler_params=pltpu.CompilerParams(vmem_limit_bytes=4 << 20),
         name="reduce_chunks",
     )(pltpu.with_memory_space_constraint(got, pltpu.VMEM))
@@ -145,11 +157,14 @@
     rank = factor_two.shape[1]
     chunks = front(slab, factor_two.T, factor_three.T).reshape(64, 1, -1)
     got = lax.all_to_all(chunks, ("z", "c", "l"), 0, 0, tiled=True, axis_index_groups=[list(range(63, -1, -1))]).reshape(-1, 128)
-    core, sent = reduce_chunks(got, 64, 32, height)
+    sent = reduce_chunks(got, 64, 32)
     every = lax.all_to_all(sent.reshape(32, 1, -1), ("h", "x", "l"), 0, 0, tiled=True, axis_index_groups=[list(range(31, -1, -1))]).reshape(-1, 128)
     terms = gram_part(every, 8, height, ("h", "x"))
-    terms = terms + lax.ppermute(terms, "c", [(0, 1), (1, 0)])
-    parts = lax.all_to_all(jnp.broadcast_to(terms[None], (8,) + terms.shape), "z", 0, 0, tiled=True, axis_index_groups=[[7, 6, 5, 4, 3, 2, 1, 0]])
+    core = core_block(sent, height, rank * rank // 64)
+    other = lax.ppermute(terms, "c", [(0, 1), (1, 0)])
+    terms, other, core = lax.optimization_barrier((terms, other, core))
+    terms = terms + other
+    parts = lax.all_to_all(jnp.broadcast_to(terms[None], (8,) + terms.shape), "z", 0, 0, tiled=True, axis_index_groups=[[7, 5, 6, 4, 3, 2, 1, 0]])
     gram = jnp.sum(parts, axis=0) / (rank * rank)
     return core, gram
 

time: 62.8 us -> 61.7 us (0.982)
  waiting for transfers between devices: 0.84 us -> 0.07 us
    ppermute x1, waiting for transfers between devices: 0.84 us -> 0.07 us  [on_device(): other = lax.ppermute(terms, 'c', [(0, 1), (1, 0)])]
    pallas_call x0 -> x1, Pallas kernels: none -> 0.76 us  [core_block(): pl.pallas_call(format_core, out_shape=jax.ShapeDtypeStruct((height, n_col...]
    pallas_call x1, Pallas kernels: 0.79 us -> 0.04 us  [reduce_chunks(): pl.pallas_call(functools.partial(gather_sum, n_parts, copies), out_shape=...]
  transfers between devices with their start and end apart: 1 -> 1, of which waited for: 1 -> 1; matrix products, arithmetic and copies ran while one was open for 0% -> 0% of each run, Pallas kernels for 0% -> 1%
where the time goes in v5:
time: 61.7 us; the launch traced here: 61 us
  blocking collectives  51.5 us (83%)
  Pallas kernels  4.27 us (7%)
  starting transfers between devices  3.92 us (6%)
  between operations  0.66 us (1%)
  other arithmetic  0.64 us (1%)
    all_to_all x1, blocking collectives, on_device(): lax.all_to_all(chunks, ('z', 'c', 'l'), 0, 0, tiled=True, axis_index_grou...  25.9 us
    all_to_all x1, blocking collectives, on_device(): lax.all_to_all(sent.reshape(32, 1, -1), ('h', 'x', 'l'), 0, 0, tiled=True...  14.6 us
    all_to_all x1, blocking collectives, on_device(): lax.all_to_all(jnp.broadcast_to(terms[None], (8,) + terms.shape), 'z', 0,...  10.9 us
    ppermute x1, starting transfers between devices, on_device(): other = lax.ppermute(terms, 'c', [(0, 1), (1, 0)])  3.92 us
    pallas_call x1, Pallas kernels, front(): pl.pallas_call(project, grid=(height // group,), in_specs=[pl.BlockSpec((...  2.89 us
  transfers between devices with their start and end apart: 1, of which 1 were waited for; matrix products, arithmetic and copies ran while one was open for 0% of the time, Pallas kernels for 1%

profile of v5, /device:TPU:1, one launch (start us, length us, event | category | flops | bytes accessed | tf_op | source)
XLA Modules:
  0.0 61.0 jit_solution(4509524520669848788)
XLA Ops:
  0.6 2.9 %project.1 = f32[576,128]{1,0:T(8,128)S(1)} custom-call(f32[32,64,256]{2,1,0:T(8,128)} %slab_ref.1, f32[48,64]{1,0:T(8,128)} %bitcast.11, f32[48,256]{1,0:T(8,128)} %bitcast.10), custom_call_target="tpu_custom_call" | custom-call | tf_op jit(solution)/shard_map/project/pallas_call | solution.py:48
  3.5 25.9 %all_to_all.15 = f32[64,1,1152]{2,1,0:T(1,128)S(1)} all-to-all(f32[64,1,1152]{2,1,0:T(1,128)S(1)} %bitcast.7), channel_id=1, replica_groups={{63,62,61,60,59,58,57,56,55,54,53,52,51,50,49,48,47,46,45,44,43,42,41,4..., dimensions={0} | all-to-all | bytes 589824 | tf_op jit(solution)/shard_map/all_to_all | solution.py:159
  29.5 14.6 %all_to_all.16 = f32[32,1,1152]{2,1,0:T(1,128)S(1)} all-to-all(f32[32,1,1152]{2,1,0:T(1,128)S(1)} %bitcast.6), channel_id=1, replica_groups={{451,450,449,448,387,386,385,384,323,322,321,320,259,258,257,256,195,19..., dimensions={0} | all-to-all | bytes 294912 | tf_op jit(solution)/shard_map/all_to_all | solution.py:161
  44.1 0.6 gram_part.1
  44.7 3.9 %collective-permute-start = (f32[32,256]{1,0:T(8,128)S(1)}, f32[32,256]{1,0:T(8,128)S(1)}, u32[]{:S(2)}, u32[]{:S(2)}) collective-permute-start(f32[32,256]{1,0:T(8,128)S(1)} %gram_part.1), channel_id=1, source_target_pairs={{0,4},{4,0},{1,5},{5,1},{2,6},{6,2},{3,7},{7,3},{8,12},{12,8},{9,1... | collective-permute-start | bytes 98312 | tf_op jit(solution)/shard_map/ppermute | solution.py:164
  48.6 0.8 %core_block.1 = f32[32,36]{1,0:T(8,128)} custom-call(f32[288,128]{1,0:T(8,128)S(1)} %reduce_chunks.1.sent_ref), custom_call_target="tpu_custom_call" | custom-call | flops 1048576 | bytes 2097152 | tf_op jit(solution)/shard_map/core_block/pallas_call | solution.py:94
  49.4 0.1 collective-permute-done
  49.5 10.9 %all_to_all.17 = f32[8,32,256]{2,1,0:T(8,128)S(1)} all-to-all(f32[8,32,256]{2,1,0:T(8,128)S(1)} %broadcast_in_dim.2), channel_id=1, replica_groups={{56,40,48,32,24,16,8,0},{57,41,49,33,25,17,9,1},{58,42,50,34,26,18,10,2..., dimensions={0} | all-to-all | bytes 524288 | tf_op jit(solution)/shard_map/all_to_all | solution.py:167
  60.4 0.6 %broadcast_multiply_fusion = f32[32,256]{1,0:T(8,128)} fusion(f32[32,256]{1,0:T(8,128)S(1)} %reduce_sum.9), kind=kLoop, calls=%fused_computation | loop fusion | flops 8192 | bytes 65536 | tf_op jit(solution)/shard_map/div | solution.py:168
  (4 shorter events, 0.1 us)
Async XLA Ops:
  44.7 4.8 %collective-permute-start = (f32[32,256]{1,0:T(8,128)S(1)}, f32[32,256]{1,0:T(8,128)S(1)}, u32[]{:S(2)}, u32[]{:S(2)}) collective-permute-start(f32[32,256]{1,0:T(8,128)S(1)} %gram_part.1), channel_id=1, source_target_pairs={{0,4},{4,0},{1,5},{5,1},{2,6},{6,2},{3,7},{7,3},{8,12},{12,8},{9,1... | collective-permute-start | bytes 98312 | tf_op jit(solution)/shard_map/ppermute | solution.py:164

commit v6 on v5

--- a/solution.py
+++ b/solution.py
@@ -35,10 +35,13 @@
     @pl.when(step == pl.num_programs(0) - 1)
     def _():
         two = two_ref[...]
-        done = exact_nt(jnp.concatenate([two[r : r + 1] for r in range(rank - 1, -1, -1)], 0), turned[...])
-        tiles = rank * height // 128
-        for t in range(tiles):
-            out_ref[pl.ds(tiles - 1 - t, rank, stride=tiles), :] = done[:, 128 * t : 128 * (t + 1)]
+        turns = [two[r : r + 1] for c in range(2) for r in range(rank - 1, -1, -1) if r // 3 % 2 == c]
+        done = exact_nt(jnp.concatenate(turns, 0), turned[...])
+        half, tiles = rank // 2, rank * height // 128
+        for c in range(2):
+            for t in range(tiles):
+                piece = done[half * c : half * (c + 1), 128 * t : 128 * (t + 1)]
+                out_ref[pl.ds(half * tiles * c + tiles - 1 - t, half, stride=tiles), :] = piece
 
 
 def front(slab, two, three, group=16):
@@ -78,7 +81,12 @@
         sent_ref[wide * b : wide * (b + 1), :] = total
 
 
-def format_core(sent_ref, core_ref, cols):
+def finish_all(scale, parts_ref, sent_ref, gram_ref, core_ref, cols):
+    n_parts = parts_ref.shape[0]
+    total = parts_ref[0]
+    for b in range(1, n_parts):
+        total = total + parts_ref[b]
+    gram_ref[...] = total * scale
     height, n_cols = core_ref.shape
     per = 128 // height
     rows = n_cols // per
@@ -90,15 +98,15 @@
     core_ref[...] = cols[...].T
 
 
-def core_block(sent, height, n_cols):
-    return pl.pallas_call(
-        format_core,
-        out_shape=jax.ShapeDtypeStruct((height, n_cols), F32),
+def finish(parts, sent, n_cols, scale):
+    height, width = parts.shape[1:]
+    return pl.pallas_call(
+        functools.partial(finish_all, scale),
+        out_shape=(jax.ShapeDtypeStruct((height, width), F32), jax.ShapeDtypeStruct((height, n_cols), F32)),
         scratch_shapes=[pltpu.VMEM((n_cols, height), F32)],
         compiler_params=pltpu.CompilerParams(vmem_limit_bytes=4 << 20),
-        cost_estimate=pl.CostEstimate(flops=1 << 20, bytes_accessed=1 << 21, transcendentals=0),
-        name="core_block",
-    )(pltpu.with_memory_space_constraint(sent, pltpu.VMEM))
+        name="finish",
+    )(*(pltpu.with_memory_space_constraint(x, pltpu.VMEM) for x in (parts, sent)))
 
 
 def reduce_chunks(got, n_parts, copies):
@@ -152,20 +160,50 @@
     )(pltpu.with_memory_space_constraint(every, pltpu.VMEM))
 
 
+def add_half(axis, both_ref, out_ref):
+    rows = out_ref.shape[0]
+    first = both_ref[0, :rows, :] + both_ref[1, :rows, :]
+    second = both_ref[0, rows:, :] + both_ref[1, rows:, :]
+    out_ref[...] = jnp.where(lax.axis_index(axis) == 0, first, second)
+
+
+def core_sum(both, axis):
+    return pl.pallas_call(
+        functools.partial(add_half, axis),
+        out_shape=pltpu.VMEM((both.shape[1] // 2, 128), F32),
+        compiler_params=pltpu.CompilerParams(vmem_limit_bytes=4 << 20),
+        name="core_sum",
+    )(pltpu.with_memory_space_constraint(both, pltpu.VMEM))
+
+
+def spread_sum(pair_ref, out_ref):
+    total = pair_ref[0] + pair_ref[1]
+    for b in range(out_ref.shape[0]):
+        out_ref[b] = total
+
+
+def pair_spread(pair, copies):
+    return pl.pallas_call(
+        spread_sum,
+        out_shape=pltpu.VMEM((copies,) + pair.shape[1:], F32),
+        compiler_params=pltpu.CompilerParams(vmem_limit_bytes=4 << 20),
+        name="pair_spread",
+    )(pltpu.with_memory_space_constraint(pair, pltpu.VMEM))
+
+
 def on_device(slab, factor_two, factor_three):
     height = slab.shape[0]
     rank = factor_two.shape[1]
-    chunks = front(slab, factor_two.T, factor_three.T).reshape(64, 1, -1)
-    got = lax.all_to_all(chunks, ("z", "c", "l"), 0, 0, tiled=True, axis_index_groups=[list(range(63, -1, -1))]).reshape(-1, 128)
-    sent = reduce_chunks(got, 64, 32)
-    every = lax.all_to_all(sent.reshape(32, 1, -1), ("h", "x", "l"), 0, 0, tiled=True, axis_index_groups=[list(range(31, -1, -1))]).reshape(-1, 128)
-    terms = gram_part(every, 8, height, ("h", "x"))
-    core = core_block(sent, height, rank * rank // 64)
-    other = lax.ppermute(terms, "c", [(0, 1), (1, 0)])
-    terms, other, core = lax.optimization_barrier((terms, other, core))
-    terms = terms + other
-    parts = lax.all_to_all(jnp.broadcast_to(terms[None], (8,) + terms.shape), "z", 0, 0, tiled=True, axis_index_groups=[[7, 5, 6, 4, 3, 2, 1, 0]])
-    gram = jnp.sum(parts, axis=0) / (rank * rank)
+    both = lax.all_gather(front(slab, factor_two.T, factor_three.T), "c", axis=0, tiled=False)
+    chunks = core_sum(both, "c").reshape(32, 1, -1)
+    down = list(range(31, -1, -1))
+    got = lax.all_to_all(chunks, ("z", "l"), 0, 0, tiled=True, axis_index_groups=[down]).reshape(-1, 128)
+    sent = reduce_chunks(got, 32, 32)
+    every = lax.all_to_all(sent.reshape(32, 1, -1), ("h", "x", "l"), 0, 0, tiled=True, axis_index_groups=[down])
+    terms = gram_part(every.reshape(-1, 128), 8, height, ("h", "x"))
+    terms = pair_spread(lax.all_gather(terms, "c", axis=0, tiled=False), 8)
+    parts = lax.all_to_all(terms, "z", 0, 0, tiled=True, axis_index_groups=[[7, 5, 6, 4, 3, 2, 1, 0]])
+    gram, core = finish(parts, sent, rank * rank // 64, 1.0 / (rank * rank))
     return core, gram
 
 

time: 61.7 us -> 59.5 us (0.964)
  starting transfers between devices: 3.92 us -> 0 us
  blocking collectives: 51.5 us -> 53.8 us
  other arithmetic: 0.64 us -> 0 us
    all_gather x0 -> x2, blocking collectives: none -> 13.1 us  [the longest x1 8.74 us: on_device(): lax.all_gather(front(slab, factor_two.T, factor_three.T), 'c', axis=0, ti...]
    all_to_all x2, blocking collectives: 36.8 us -> 26.6 us  [the longest x1 15.9 us: on_device(): lax.all_to_all(chunks, ('z', 'l'), 0, 0, tiled=True, axis_index_groups=[d...]
    ppermute x1 -> x0, starting transfers between devices: 3.92 us -> none  [on_device(): other = lax.ppermute(terms, 'c', [(0, 1), (1, 0)])]
    div x1 -> x0, other arithmetic: 0.62 us -> none  [on_device(): gram = jnp.sum(parts, axis=0) / (rank * rank)]
  transfers between devices with their start and end apart: 1 -> 0, of which waited for: 1 -> 0; matrix products, arithmetic and copies ran while one was open for 0% -> 0% of each run, Pallas kernels for 1% -> 0%
where the time goes in v6:
time: 59.5 us; the launch traced here: 58.7 us
  blocking collectives  53.8 us (90%)
  Pallas kernels  4.32 us (7%)
  between operations  0.65 us (1%)
    all_to_all x1, blocking collectives, on_device(): lax.all_to_all(chunks, ('z', 'l'), 0, 0, tiled=True, axis_index_groups=[d...  15.9 us
    all_to_all x1, blocking collectives, on_device(): lax.all_to_all(sent.reshape(32, 1, -1), ('h', 'x', 'l'), 0, 0, tiled=True...  14 us
    all_to_all x1, blocking collectives, on_device(): lax.all_to_all(terms, 'z', 0, 0, tiled=True, axis_index_groups=[[7, 5, 6,...  10.8 us
    all_gather x1, blocking collectives, on_device(): lax.all_gather(front(slab, factor_two.T, factor_three.T), 'c', axis=0, ti...  8.74 us
    all_gather x1, blocking collectives, on_device(): terms = pair_spread(lax.all_gather(terms, 'c', axis=0, tiled=False), 8)  4.37 us
    pallas_call x1, Pallas kernels, front(): pl.pallas_call(project, grid=(height // group,), in_specs=[pl.BlockSpec((...  2.89 us

profile of v6, /device:TPU:1, one launch (start us, length us, event | category | flops | bytes accessed | tf_op | source)
XLA Modules:
  0.0 58.7 jit_solution(16671574229593023828)
XLA Ops:
  0.6 2.9 %project.1 = f32[576,128]{1,0:T(8,128)S(1)} custom-call(f32[32,64,256]{2,1,0:T(8,128)} %slab_ref.1, f32[48,64]{1,0:T(8,128)} %bitcast.15, f32[48,256]{1,0:T(8,128)} %bitcast.14), custom_call_target="tpu_custom_call" | custom-call | tf_op jit(solution)/shard_map/project/pallas_call | solution.py:51
  3.5 8.7 %all-gather = f32[1152,128]{1,0:T(8,128)S(1)} all-gather(f32[576,128]{1,0:T(8,128)S(1)} %project.1), channel_id=2, replica_groups=mesh['h'=2,'x'=4,'z'=8,'c'=2,'l'=4] {'c'}, dimensions={0}, use_global_device_ids=true | all-gather | bytes 884736 | tf_op jit(solution)/shard_map/all_gather | solution.py:197
  12.3 15.9 %all_to_all.15 = f32[32,1,1152]{2,1,0:T(1,128)S(1)} all-to-all(f32[32,1,1152]{2,1,0:T(1,128)S(1)} %bitcast.12), channel_id=1, replica_groups={{59,58,57,56,51,50,49,48,43,42,41,40,35,34,33,32,27,26,25,24,19,18,17,1..., dimensions={0} | all-to-all | bytes 294912 | tf_op jit(solution)/shard_map/all_to_all | solution.py:200
  28.2 14.0 %all_to_all.16 = f32[32,1,1152]{2,1,0:T(1,128)S(1)} all-to-all(f32[32,1,1152]{2,1,0:T(1,128)S(1)} %bitcast.9), channel_id=1, replica_groups={{451,450,449,448,387,386,385,384,323,322,321,320,259,258,257,256,195,19..., dimensions={0} | all-to-all | bytes 294912 | tf_op jit(solution)/shard_map/all_to_all | solution.py:202
  42.2 0.6 gram_part.1
  42.8 4.4 %all-gather.1 = f32[64,256]{1,0:T(8,128)S(1)} all-gather(f32[32,256]{1,0:T(8,128)S(1)} %gram_part.1), channel_id=3, replica_groups=mesh['h'=2,'x'=4,'z'=8,'c'=2,'l'=4] {'c'}, dimensions={0}, use_global_device_ids=true | all-gather | bytes 98304 | tf_op jit(solution)/shard_map/all_gather | solution.py:204
  47.2 10.8 %all_to_all.17.parts_ref = f32[8,32,256]{2,1,0:T(8,128)S(1)} all-to-all(f32[8,32,256]{2,1,0:T(8,128)S(1)} %pair_spread.1), channel_id=1, replica_groups={{56,40,48,32,24,16,8,0},{57,41,49,33,25,17,9,1},{58,42,50,34,26,18,10,2..., dimensions={0} | all-to-all | bytes 524288 | tf_op jit(solution)/shard_map/all_to_all | solution.py:205
  58.0 0.8 %finish.1 = (f32[32,256]{1,0:T(8,128)}, f32[32,36]{1,0:T(8,128)}) custom-call(f32[8,32,256]{2,1,0:T(8,128)S(1)} %all_to_all.17.parts_ref, f32[288,128]{1,0:T(8,128)S(1)} %reduce_chunks.1.sent_ref), custom_call_target="tpu_custom_call" | custom-call | tf_op jit(solution)/shard_map/finish/pallas_call | solution.py:103
  (3 shorter events, 0.1 us)

commit v7 on v6

--- a/solution.py
+++ b/solution.py
@@ -13,6 +13,11 @@
 def halves(x):
     high = x.astype(BF16)
     return high, (x - high.astype(F32)).astype(BF16)
+
+
+def rounded(x):
+    high = x.astype(BF16).astype(F32)
+    return high, x - high
 
 
 def exact_nt(left, right):
@@ -128,14 +133,17 @@
     mine = jnp.zeros_like(blocks[0])
     for a in range(n_rows):
         mine = jnp.where(me == a, blocks[a], mine)
-    lh, ll = halves(mine.T)
-    rh, rl = halves(jnp.concatenate(blocks, 1))
-    both = jnp.dot(jnp.concatenate([lh, ll], 0), rh, preferred_element_type=F32)
-    low = jnp.dot(lh, rl, preferred_element_type=F32)
+    lh, ll = rounded(mine)
+    rh, rl = rounded(jnp.concatenate(blocks, 1))
+    gap = jnp.zeros((-deep % 8, 128), F32)
+    left = jnp.concatenate([lh, gap, ll, gap, lh, gap], 0).T.astype(BF16)
+    gap = jnp.zeros((-deep % 8, rh.shape[1]), F32)
+    right = jnp.concatenate([rh, gap, rh, gap, rl, gap], 0).astype(BF16)
+    both = jnp.dot(left, right, preferred_element_type=F32)
     lane = lax.broadcasted_iota(jnp.int32, (height, 128), 1) // height
     folded = []
     for a in range(n_rows):
-        z = both[:128, 128 * a : 128 * (a + 1)] + both[128:, 128 * a : 128 * (a + 1)] + low[:, 128 * a : 128 * (a + 1)]
+        z = both[:, 128 * a : 128 * (a + 1)]
         u = jnp.zeros((height, 128), F32)
         for q in range(per):
             u = jnp.where(lane == q, z[height * q : height * (q + 1), :], u)
@@ -202,7 +210,7 @@
     every = lax.all_to_all(sent.reshape(32, 1, -1), ("h", "x", "l"), 0, 0, tiled=True, axis_index_groups=[down])
     terms = gram_part(every.reshape(-1, 128), 8, height, ("h", "x"))
     terms = pair_spread(lax.all_gather(terms, "c", axis=0, tiled=False), 8)
-    parts = lax.all_to_all(terms, "z", 0, 0, tiled=True, axis_index_groups=[[7, 5, 6, 4, 3, 2, 1, 0]])
+    parts = lax.all_to_all(terms, "z", 0, 0, tiled=True, axis_index_groups=[[6, 7, 5, 4, 2, 3, 1, 0]])
     gram, core = finish(parts, sent, rank * rank // 64, 1.0 / (rank * rank))
     return core, gram
 

time: 59.5 us -> 59 us (level)
  no operation moved by 1% of the time
where the time goes in v7:
time: 59 us; the launch traced here: 58.4 us
  blocking collectives  53.6 us (91%)
  Pallas kernels  4.18 us (7%)
  between operations  0.66 us (1%)
    all_to_all x1, blocking collectives, on_device(): lax.all_to_all(chunks, ('z', 'l'), 0, 0, tiled=True, axis_index_groups=[d...  15.9 us
    all_to_all x1, blocking collectives, on_device(): lax.all_to_all(sent.reshape(32, 1, -1), ('h', 'x', 'l'), 0, 0, tiled=True...  14 us
    all_to_all x1, blocking collectives, on_device(): lax.all_to_all(terms, 'z', 0, 0, tiled=True, axis_index_groups=[[6, 7, 5,...  10.5 us
    all_gather x1, blocking collectives, on_device(): lax.all_gather(front(slab, factor_two.T, factor_three.T), 'c', axis=0, ti...  8.74 us
    all_gather x1, blocking collectives, on_device(): terms = pair_spread(lax.all_gather(terms, 'c', axis=0, tiled=False), 8)  4.37 us
    pallas_call x1, Pallas kernels, front(): pl.pallas_call(project, grid=(height // group,), in_specs=[pl.BlockSpec((...  2.89 us

profile of v7, /device:TPU:1, one launch (start us, length us, event | category | flops | bytes accessed | tf_op | source)
XLA Modules:
  0.0 58.4 jit_solution(3953652339063117235)
XLA Ops:
  0.6 2.9 %project.1 = f32[576,128]{1,0:T(8,128)S(1)} custom-call(f32[32,64,256]{2,1,0:T(8,128)} %slab_ref.1, f32[48,64]{1,0:T(8,128)} %bitcast.15, f32[48,256]{1,0:T(8,128)} %bitcast.14), custom_call_target="tpu_custom_call" | custom-call | tf_op jit(solution)/shard_map/project/pallas_call | solution.py:56
  3.5 8.7 %all-gather = f32[1152,128]{1,0:T(8,128)S(1)} all-gather(f32[576,128]{1,0:T(8,128)S(1)} %project.1), channel_id=2, replica_groups=mesh['h'=2,'x'=4,'z'=8,'c'=2,'l'=4] {'c'}, dimensions={0}, use_global_device_ids=true | all-gather | bytes 884736 | tf_op jit(solution)/shard_map/all_gather | solution.py:205
  12.3 15.9 %all_to_all.15 = f32[32,1,1152]{2,1,0:T(1,128)S(1)} all-to-all(f32[32,1,1152]{2,1,0:T(1,128)S(1)} %bitcast.12), channel_id=1, replica_groups={{59,58,57,56,51,50,49,48,43,42,41,40,35,34,33,32,27,26,25,24,19,18,17,1..., dimensions={0} | all-to-all | bytes 294912 | tf_op jit(solution)/shard_map/all_to_all | solution.py:208
  28.2 14.0 %all_to_all.16 = f32[32,1,1152]{2,1,0:T(1,128)S(1)} all-to-all(f32[32,1,1152]{2,1,0:T(1,128)S(1)} %bitcast.9), channel_id=1, replica_groups={{451,450,449,448,387,386,385,384,323,322,321,320,259,258,257,256,195,19..., dimensions={0} | all-to-all | bytes 294912 | tf_op jit(solution)/shard_map/all_to_all | solution.py:210
  42.2 0.4 gram_part.1
  42.7 4.4 %all-gather.1 = f32[64,256]{1,0:T(8,128)S(1)} all-gather(f32[32,256]{1,0:T(8,128)S(1)} %gram_part.1), channel_id=3, replica_groups=mesh['h'=2,'x'=4,'z'=8,'c'=2,'l'=4] {'c'}, dimensions={0}, use_global_device_ids=true | all-gather | bytes 98304 | tf_op jit(solution)/shard_map/all_gather | solution.py:212
  47.1 10.5 %all_to_all.17.parts_ref = f32[8,32,256]{2,1,0:T(8,128)S(1)} all-to-all(f32[8,32,256]{2,1,0:T(8,128)S(1)} %pair_spread.1), channel_id=1, replica_groups={{48,56,40,32,16,24,8,0},{49,57,41,33,17,25,9,1},{50,58,42,34,18,26,10,2..., dimensions={0} | all-to-all | bytes 524288 | tf_op jit(solution)/shard_map/all_to_all | solution.py:213
  57.6 0.8 %finish.1 = (f32[32,256]{1,0:T(8,128)}, f32[32,36]{1,0:T(8,128)}) custom-call(f32[8,32,256]{2,1,0:T(8,128)S(1)} %all_to_all.17.parts_ref, f32[288,128]{1,0:T(8,128)S(1)} %reduce_chunks.1.sent_ref), custom_call_target="tpu_custom_call" | custom-call | tf_op jit(solution)/shard_map/finish/pallas_call | solution.py:108
  (3 shorter events, 0.1 us)

commit v8 on v7

--- a/solution.py
+++ b/solution.py
@@ -8,6 +8,7 @@
 
 F32, BF16 = jnp.float32, jnp.bfloat16
 NT = (((1,), (1,)), ((), ()))
+SECOND = (7, 6, 5, 4, 3, 2, 1, 0)
 
 
 def halves(x):
@@ -129,7 +130,11 @@
     me = lax.axis_index(axes)
     per = 128 // height
     deep = all_ref.shape[0] // n_rows
-    blocks = [all_ref[deep * a : deep * (a + 1), :] for a in range(n_rows)][::-1]
+    at = [deep * SECOND.index(a) for a in range(n_rows)]
+    blocks = [all_ref[s : s + deep, :] for s in at]
+    piece = deep // 4
+    for a in range(4, n_rows):
+        blocks[a] = jnp.concatenate([blocks[a][piece * l : piece * (l + 1), :] for l in (3, 2, 1, 0)], 0)
     mine = jnp.zeros_like(blocks[0])
     for a in range(n_rows):
         mine = jnp.where(me == a, blocks[a], mine)
@@ -207,7 +212,8 @@
     down = list(range(31, -1, -1))
     got = lax.all_to_all(chunks, ("z", "l"), 0, 0, tiled=True, axis_index_groups=[down]).reshape(-1, 128)
     sent = reduce_chunks(got, 32, 32)
-    every = lax.all_to_all(sent.reshape(32, 1, -1), ("h", "x", "l"), 0, 0, tiled=True, axis_index_groups=[down])
+    second = [4 * a + l for a in SECOND for l in ((0, 1, 2, 3) if a > 3 else (3, 2, 1, 0))]
+    every = lax.all_to_all(sent.reshape(32, 1, -1), ("h", "x", "l"), 0, 0, tiled=True, axis_index_groups=[second])
     terms = gram_part(every.reshape(-1, 128), 8, height, ("h", "x"))
     terms = pair_spread(lax.all_gather(terms, "c", axis=0, tiled=False), 8)
     parts = lax.all_to_all(terms, "z", 0, 0, tiled=True, axis_index_groups=[[6, 7, 5, 4, 2, 3, 1, 0]])

time: 59 us -> 58.7 us (level)
    all_to_all x1, blocking collectives: 14 us -> 13.2 us  [on_device(): lax.all_to_all(sent.reshape(32, 1, -1), ('h', 'x', 'l'), 0, 0, tiled=True...]
where the time goes in v8:
time: 58.7 us; the launch traced here: 58.2 us
  blocking collectives  53.4 us (91%)
  Pallas kernels  4.18 us (7%)
  between operations  0.66 us (1%)
    all_to_all x1, blocking collectives, on_device(): lax.all_to_all(chunks, ('z', 'l'), 0, 0, tiled=True, axis_index_groups=[d...  15.9 us
    all_to_all x1, blocking collectives, on_device(): lax.all_to_all(sent.reshape(32, 1, -1), ('h', 'x', 'l'), 0, 0, tiled=True...  13.2 us
    all_to_all x1, blocking collectives, on_device(): lax.all_to_all(terms, 'z', 0, 0, tiled=True, axis_index_groups=[[6, 7, 5,...  10.7 us
    all_gather x1, blocking collectives, on_device(): lax.all_gather(front(slab, factor_two.T, factor_three.T), 'c', axis=0, ti...  8.74 us
    all_gather x1, blocking collectives, on_device(): terms = pair_spread(lax.all_gather(terms, 'c', axis=0, tiled=False), 8)  4.93 us
    pallas_call x1, Pallas kernels, front(): pl.pallas_call(project, grid=(height // group,), in_specs=[pl.BlockSpec((...  2.89 us

profile of v8, /device:TPU:1, one launch (start us, length us, event | category | flops | bytes accessed | tf_op | source)
XLA Modules:
  0.0 58.2 jit_solution(1613095479380532266)
XLA Ops:
  0.6 2.9 %project.1 = f32[576,128]{1,0:T(8,128)S(1)} custom-call(f32[32,64,256]{2,1,0:T(8,128)} %slab_ref.1, f32[48,64]{1,0:T(8,128)} %bitcast.15, f32[48,256]{1,0:T(8,128)} %bitcast.14), custom_call_target="tpu_custom_call" | custom-call | tf_op jit(solution)/shard_map/project/pallas_call | solution.py:57
  3.5 8.7 %all-gather = f32[1152,128]{1,0:T(8,128)S(1)} all-gather(f32[576,128]{1,0:T(8,128)S(1)} %project.1), channel_id=2, replica_groups=mesh['h'=2,'x'=4,'z'=8,'c'=2,'l'=4] {'c'}, dimensions={0}, use_global_device_ids=true | all-gather | bytes 884736 | tf_op jit(solution)/shard_map/all_gather | solution.py:210
  12.3 15.9 %all_to_all.15 = f32[32,1,1152]{2,1,0:T(1,128)S(1)} all-to-all(f32[32,1,1152]{2,1,0:T(1,128)S(1)} %bitcast.12), channel_id=1, replica_groups={{59,58,57,56,51,50,49,48,43,42,41,40,35,34,33,32,27,26,25,24,19,18,17,1..., dimensions={0} | all-to-all | bytes 294912 | tf_op jit(solution)/shard_map/all_to_all | solution.py:213
  28.2 13.2 %all_to_all.16 = f32[32,1,1152]{2,1,0:T(1,128)S(1)} all-to-all(f32[32,1,1152]{2,1,0:T(1,128)S(1)} %bitcast.9), channel_id=1, replica_groups={{448,449,450,451,384,385,386,387,320,321,322,323,256,257,258,259,195,19..., dimensions={0} | all-to-all | bytes 294912 | tf_op jit(solution)/shard_map/all_to_all | solution.py:216
  41.4 0.4 gram_part.1
  41.8 4.9 %all-gather.1 = f32[64,256]{1,0:T(8,128)S(1)} all-gather(f32[32,256]{1,0:T(8,128)S(1)} %gram_part.1), channel_id=3, replica_groups=mesh['h'=2,'x'=4,'z'=8,'c'=2,'l'=4] {'c'}, dimensions={0}, use_global_device_ids=true | all-gather | bytes 98304 | tf_op jit(solution)/shard_map/all_gather | solution.py:218
  46.8 10.7 %all_to_all.17.parts_ref = f32[8,32,256]{2,1,0:T(8,128)S(1)} all-to-all(f32[8,32,256]{2,1,0:T(8,128)S(1)} %pair_spread.1), channel_id=1, replica_groups={{48,56,40,32,16,24,8,0},{49,57,41,33,17,25,9,1},{50,58,42,34,18,26,10,2..., dimensions={0} | all-to-all | bytes 524288 | tf_op jit(solution)/shard_map/all_to_all | solution.py:219
  57.5 0.8 %finish.1 = (f32[32,256]{1,0:T(8,128)}, f32[32,36]{1,0:T(8,128)}) custom-call(f32[8,32,256]{2,1,0:T(8,128)S(1)} %all_to_all.17.parts_ref, f32[288,128]{1,0:T(8,128)S(1)} %reduce_chunks.1.sent_ref), custom_call_target="tpu_custom_call" | custom-call | tf_op jit(solution)/shard_map/finish/pallas_call | solution.py:109
  (3 shorter events, 0.1 us)

commit v9 on v8

--- a/solution.py
+++ b/solution.py
@@ -29,7 +29,7 @@
     return both[:m] + both[m:] + lax.dot_general(lh, rl, NT, preferred_element_type=F32)
 
 
-def project(slab_ref, two_ref, three_ref, out_ref, turned):
+def project(slab_ref, two_ref, three_ref, keep_ref, send_ref, turned):
     step = pl.program_id(0)
     group, across, depth = slab_ref.shape
     rank = two_ref.shape[0]
@@ -44,16 +44,18 @@
         turns = [two[r : r + 1] for c in range(2) for r in range(rank - 1, -1, -1) if r // 3 % 2 == c]
         done = exact_nt(jnp.concatenate(turns, 0), turned[...])
         half, tiles = rank // 2, rank * height // 128
-        for c in range(2):
-            for t in range(tiles):
-                piece = done[half * c : half * (c + 1), 128 * t : 128 * (t + 1)]
-                out_ref[pl.ds(half * tiles * c + tiles - 1 - t, half, stride=tiles), :] = piece
+        first_core = lax.axis_index("c") == 0
+        keep = jnp.where(first_core, done[:half], done[half:])
+        send = jnp.where(first_core, done[half:], done[:half])
+        for t in range(tiles):
+            keep_ref[pl.ds(tiles - 1 - t, half, stride=tiles), :] = keep[:, 128 * t : 128 * (t + 1)]
+            send_ref[pl.ds(tiles - 1 - t, half, stride=tiles), :] = send[:, 128 * t : 128 * (t + 1)]
 
 
 def front(slab, two, three, group=16):
     height, across, depth = slab.shape
     rank = two.shape[0]
-    rows = rank * rank * height // 128
+    rows = rank * rank * height // 256
     return pl.pallas_call(
         project,
         grid=(height // group,),
@@ -62,8 +64,8 @@
             pl.BlockSpec((rank, across), lambda g: (0, 0)),
             pl.BlockSpec((rank, depth), lambda g: (0, 0)),
         ],
-        out_specs=pl.BlockSpec((rows, 128), lambda g: (0, 0)),
-        out_shape=pltpu.VMEM((rows, 128), F32),
+        out_specs=[pl.BlockSpec((rows, 128), lambda g: (0, 0))] * 2,
+        out_shape=[pltpu.VMEM((rows, 128), F32)] * 2,
         scratch_shapes=[pltpu.VMEM((rank * height, across), F32)],
         compiler_params=pltpu.CompilerParams(vmem_limit_bytes=16 << 20),
         name="project",
@@ -173,20 +175,18 @@
     )(pltpu.with_memory_space_constraint(every, pltpu.VMEM))
 
 
-def add_half(axis, both_ref, out_ref):
-    rows = out_ref.shape[0]
-    first = both_ref[0, :rows, :] + both_ref[1, :rows, :]
-    second = both_ref[0, rows:, :] + both_ref[1, rows:, :]
-    out_ref[...] = jnp.where(lax.axis_index(axis) == 0, first, second)
-
-
-def core_sum(both, axis):
-    return pl.pallas_call(
-        functools.partial(add_half, axis),
-        out_shape=pltpu.VMEM((both.shape[1] // 2, 128), F32),
+def add_other(axis, keep_ref, both_ref, out_ref):
+    other = jnp.where(lax.axis_index(axis) == 0, both_ref[1], both_ref[0])
+    out_ref[...] = keep_ref[...] + other
+
+
+def core_sum(keep, both, axis):
+    return pl.pallas_call(
+        functools.partial(add_other, axis),
+        out_shape=pltpu.VMEM(keep.shape, F32),
         compiler_params=pltpu.CompilerParams(vmem_limit_bytes=4 << 20),
         name="core_sum",
-    )(pltpu.with_memory_space_constraint(both, pltpu.VMEM))
+    )(*(pltpu.with_memory_space_constraint(x, pltpu.VMEM) for x in (keep, both)))
 
 
 def spread_sum(pair_ref, out_ref):
@@ -207,8 +207,8 @@
 def on_device(slab, factor_two, factor_three):
     height = slab.shape[0]
     rank = factor_two.shape[1]
-    both = lax.all_gather(front(slab, factor_two.T, factor_three.T), "c", axis=0, tiled=False)
-    chunks = core_sum(both, "c").reshape(32, 1, -1)
+    keep, send = front(slab, factor_two.T, factor_three.T)
+    chunks = core_sum(keep, lax.all_gather(send, "c", axis=0, tiled=False), "c").reshape(32, 1, -1)
     down = list(range(31, -1, -1))
     got = lax.all_to_all(chunks, ("z", "l"), 0, 0, tiled=True, axis_index_groups=[down]).reshape(-1, 128)
     sent = reduce_chunks(got, 32, 32)

time: 58.7 us -> 58.5 us (level)
  no operation moved by 1% of the time
where the time goes in v9:
time: 58.5 us; the launch traced here: 58 us
  blocking collectives  53.2 us (91%)
  Pallas kernels  4.18 us (7%)
  between operations  0.66 us (1%)
    all_to_all x1, blocking collectives, on_device(): lax.all_to_all(chunks, ('z', 'l'), 0, 0, tiled=True, axis_index_groups=[d...  15.9 us
    all_to_all x1, blocking collectives, on_device(): lax.all_to_all(sent.reshape(32, 1, -1), ('h', 'x', 'l'), 0, 0, tiled=True...  13.2 us
    all_to_all x1, blocking collectives, on_device(): lax.all_to_all(terms, 'z', 0, 0, tiled=True, axis_index_groups=[[6, 7, 5,...  10.7 us
    all_gather x1, blocking collectives, on_device(): lax.all_gather(send, 'c', axis=0, tiled=False)  8.54 us
    all_gather x1, blocking collectives, on_device(): terms = pair_spread(lax.all_gather(terms, 'c', axis=0, tiled=False), 8)  4.92 us
    pallas_call x1, Pallas kernels, front(): pl.pallas_call(project, grid=(height // group,), in_specs=[pl.BlockSpec((...  2.9 us

profile of v9, /device:TPU:1, one launch (start us, length us, event | category | flops | bytes accessed | tf_op | source)
XLA Modules:
  0.0 58.0 jit_solution(10840671068190043165)
XLA Ops:
  0.6 2.9 %project.1 = (f32[288,128]{1,0:T(8,128)S(1)}, f32[288,128]{1,0:T(8,128)S(1)}) custom-call(f32[32,64,256]{2,1,0:T(8,128)} %slab_ref.1, f32[48,64]{1,0:T(8,128)} %bitcast.15, f32[48,256]{1,0:T(8,128)} %bitcast.14), custom_call_target="tpu_custom_call" | custom-call | tf_op jit(solution)/shard_map/project/pallas_call | solution.py:59
  3.5 8.5 %all-gather = f32[576,128]{1,0:T(8,128)S(1)} all-gather(f32[288,128]{1,0:T(8,128)S(1)} %get-tuple-element.7), channel_id=2, replica_groups=mesh['h'=2,'x'=4,'z'=8,'c'=2,'l'=4] {'c'}, dimensions={0}, use_global_device_ids=true | all-gather | bytes 442368 | tf_op jit(solution)/shard_map/all_gather | solution.py:211
  12.1 15.9 %all_to_all.15 = f32[32,1,1152]{2,1,0:T(1,128)S(1)} all-to-all(f32[32,1,1152]{2,1,0:T(1,128)S(1)} %bitcast.12), channel_id=1, replica_groups={{59,58,57,56,51,50,49,48,43,42,41,40,35,34,33,32,27,26,25,24,19,18,17,1..., dimensions={0} | all-to-all | bytes 294912 | tf_op jit(solution)/shard_map/all_to_all | solution.py:213
  28.0 13.2 %all_to_all.16 = f32[32,1,1152]{2,1,0:T(1,128)S(1)} all-to-all(f32[32,1,1152]{2,1,0:T(1,128)S(1)} %bitcast.8), channel_id=1, replica_groups={{448,449,450,451,384,385,386,387,320,321,322,323,256,257,258,259,195,19..., dimensions={0} | all-to-all | bytes 294912 | tf_op jit(solution)/shard_map/all_to_all | solution.py:216
  41.2 0.4 gram_part.1
  41.6 4.9 %all-gather.1 = f32[64,256]{1,0:T(8,128)S(1)} all-gather(f32[32,256]{1,0:T(8,128)S(1)} %gram_part.1), channel_id=3, replica_groups=mesh['h'=2,'x'=4,'z'=8,'c'=2,'l'=4] {'c'}, dimensions={0}, use_global_device_ids=true | all-gather | bytes 98304 | tf_op jit(solution)/shard_map/all_gather | solution.py:218
  46.6 10.7 %all_to_all.17.parts_ref = f32[8,32,256]{2,1,0:T(8,128)S(1)} all-to-all(f32[8,32,256]{2,1,0:T(8,128)S(1)} %pair_spread.1), channel_id=1, replica_groups={{48,56,40,32,16,24,8,0},{49,57,41,33,17,25,9,1},{50,58,42,34,18,26,10,2..., dimensions={0} | all-to-all | bytes 524288 | tf_op jit(solution)/shard_map/all_to_all | solution.py:219
  57.3 0.8 %finish.1 = (f32[32,256]{1,0:T(8,128)}, f32[32,36]{1,0:T(8,128)}) custom-call(f32[8,32,256]{2,1,0:T(8,128)S(1)} %all_to_all.17.parts_ref, f32[288,128]{1,0:T(8,128)S(1)} %reduce_chunks.1.sent_ref), custom_call_target="tpu_custom_call" | custom-call | tf_op jit(solution)/shard_map/finish/pallas_call | solution.py:111
  (3 shorter events, 0.1 us)
